TPU v7x, 128 devices: a whole 4x4x4 slice. The times are simulated.
128 devices in a mesh: tok: 4 (over y), vocab: 32 (over x, z, core).
Axes of the slice: x: 4, y: 4, z: 4, core: 2. Of those that a mesh axis runs over, the one named last changes fastest.
Arguments:
- teacher_logits: bfloat16 [512, 131072], P('tok', 'vocab'), may hold values from -18 to 240
- hidden: bfloat16 [512, 4608], P('tok'), may hold values from -6 to 6
- new_head: bfloat16 [4608, 131072], P(None, ('tok', 'vocab')), may hold values from -0.26516504 to 0.26516504
- labels: int32 [512], replicated, may hold values from 0 to 131071
- map_target: int32 [1024, 4], P('vocab'), may hold values from 0 to 1023, as said below
- map_weight: bfloat16 [1024, 4, 128, 128], P('vocab'), may hold values from 0 to 0.017578125, as said below
Outputs:
- loss: float32 [512], P('tok')
- head_grad: bfloat16 [4608, 131072], P(None, ('tok', 'vocab'))
Inputs may be any that keep to these rules, and one draw needn't show every extreme that they name: `map_target`: values are ids of new blocks; new block b belongs to the device at index b // 8 of tok and vocab together, tok first. Of the 128 entries of one vocab index, at most 2 belong to one device, and some device gets exactly 2. `map_weight`: entries are non-negative.
All inputs are finite; a program needn't handle non-finite values.
Results may differ from a plain program's by a relative error of at most 0.001.
The roundings to bfloat16 on the way count: a program that leaves them out, or rounds other values in their place, can miss the bound.
Values may be sent and summed in bfloat16 or wider, within the bound.
A program may use at most 128 MiB of HBM per device.

v0:
```python
import jax
import jax.numpy as jnp
from jax import lax
from jax.sharding import PartitionSpec as P


def local(teacher_logits, hidden, new_head, labels, map_target, map_weight):
    tok_rows = teacher_logits.shape[0]
    block = map_weight.shape[2]
    fanout = map_weight.shape[1]
    old_blocks = map_target.shape[0]
    entries = old_blocks * fanout
    n_tok = lax.axis_size("tok")
    n_vocab = lax.axis_size("vocab")
    nodes = n_tok * n_vocab
    capacity = max(2, 2 * entries // nodes)
    new_cols = new_head.shape[1]
    per_node = new_cols // block
    own_index = lax.axis_index(("tok", "vocab"))
    scores = teacher_logits.astype(jnp.float32)
    local_top = jnp.max(scores, axis=1)
    highest = lax.pmax(local_top, "vocab")
    total = lax.psum(jnp.sum(jnp.exp(scores - highest[:, None]), axis=1), "vocab")
    teacher_prob = (jnp.exp(scores - highest[:, None]) / total[:, None]).astype(jnp.bfloat16)
    pieces = teacher_prob.reshape(tok_rows, old_blocks, block)
    contrib = jnp.einsum("tjb,jkbc->jktc", pieces, map_weight, preferred_element_type=jnp.float32)
    contrib = contrib.astype(jnp.bfloat16).reshape(entries, tok_rows, block)
    owners = (map_target // per_node).reshape(entries)
    earlier = jnp.arange(entries)[None, :] < jnp.arange(entries)[:, None]
    slots = jnp.sum((owners[:, None] == owners[None, :]) & earlier, axis=1)
    outbox = (
        jnp.zeros((nodes, capacity, tok_rows, block), jnp.bfloat16).at[owners, slots].set(contrib)
    )
    inbox = lax.all_to_all(outbox, ("tok", "vocab"), split_axis=0, concat_axis=0, tiled=True)
    inbox = inbox.reshape(n_tok, n_vocab, capacity, tok_rows, block)
    targets_all = lax.all_gather(map_target, "vocab", axis=0, tiled=True).reshape(n_vocab, entries)
    owners_all = targets_all // per_node
    local_block = targets_all % per_node
    slots_all = jnp.sum((owners_all[:, :, None] == owners_all[:, None, :]) & earlier[None], axis=2)
    picked = (owners_all == own_index)[:, :, None] & (
        slots_all[:, :, None] == jnp.arange(capacity)[None, None, :]
    )
    block_hit = local_block[:, :, None] == jnp.arange(per_node)[None, None, :]
    landing = jnp.einsum(
        "vec,veb->vcb", picked.astype(jnp.float32), block_hit.astype(jnp.float32)
    ).astype(jnp.bfloat16)
    target = jnp.einsum("vcb,svctk->stbk", landing, inbox, preferred_element_type=jnp.float32)
    target = target.reshape(n_tok * tok_rows, new_cols)
    everyone = lax.all_gather(hidden, "tok", axis=0, tiled=True)
    logits = jnp.dot(everyone, new_head, preferred_element_type=jnp.float32)
    columns = own_index * new_cols + jnp.arange(new_cols, dtype=jnp.int32)
    label_hit = labels[:, None] == columns[None, :]
    label_part = jnp.sum(jnp.where(label_hit, logits, 0.0), axis=1)
    mass_part = jnp.sum(target, axis=1)
    inner_part = jnp.sum(target * logits, axis=1)
    row_top = jnp.max(logits, axis=1)
    top_all = lax.pmax(row_top, ("tok", "vocab"))
    exp_part = jnp.sum(jnp.exp(logits - top_all[:, None]), axis=1)
    total_all, target_mass, inner, label_logit = lax.psum(
        (exp_part, mass_part, inner_part, label_part), ("tok", "vocab")
    )
    log_total = top_all + jnp.log(total_all)
    loss_all = target_mass * log_total - inner + log_total - label_logit
    loss = lax.dynamic_slice_in_dim(loss_all, lax.axis_index("tok") * tok_rows, tok_rows)
    probs = jnp.exp(logits - log_total[:, None])
    grad_logits = (
        (target_mass + 1.0)[:, None] * probs - target - label_hit.astype(jnp.float32)
    ).astype(jnp.bfloat16)
    head_grad = lax.dot_general(
        everyone, grad_logits, (((0,), (0,)), ((), ())), preferred_element_type=jnp.float32
    )
    return (loss, head_grad.astype(jnp.bfloat16))


def solution(mesh):
    return jax.shard_map(
        local,
        mesh=mesh,
        in_specs=(
            P("tok", "vocab"),
            P("tok", None),
            P(None, ("tok", "vocab")),
            P(),
            P("vocab", None),
            P("vocab", None, None, None),
        ),
        out_specs=(P("tok"), P(None, ("tok", "vocab"))),
        check_vma=False,
    )
```

profile of v0, /device:TPU:1, one launch (start us, length us, event | category | flops | bytes accessed | tf_op | source)
XLA Modules:
  0.0 477.8 jit_solution(10782458382185194525)
XLA Ops:
  7.2 0.7 all-gather.3.cloned.1.call-update
  7.9 0.7 add_select_fusion.2
  8.9 1.5 reduce_max.23
  10.4 64.8 %pmax.14 = f32[128]{0:T(128)S(1)} all-reduce(bf16[128]{0:T(256)(128)(2,1)S(1)} %reduce_max.23), channel_id=1, replica_groups=mesh['tok'=4,'vocab'=32] {'vocab'}, use_global_device_ids=true, to_apply=%region_2.0 | all-reduce | flops 128 | bytes 768 | tf_op jit(solution)/shard_map/pmax | solution.py:22
  75.2 0.5 fusion.7
  75.7 67.0 %psum.35 = f32[128]{0:T(128)S(1)} all-reduce(f32[128]{0:T(128)S(1)} %fusion.7), channel_id=1, replica_groups=mesh['tok'=4,'vocab'=32] {'vocab'}, use_global_device_ids=true, to_apply=%region_4.5 | all-reduce | flops 128 | bytes 1024 | tf_op jit(solution)/shard_map/psum | solution.py:23
  142.7 0.5 fusion.9
  143.2 0.2 copy.62
  143.5 0.2 convert_reduce_fusion.1
  143.6 1.3 copy-done.2
  144.9 3.2 convolution_convert_fusion.1
  148.1 5.5 %broadcast_in_dim.5 = bf16[128,2,128,128]{3,2,1,0:T(8,128)(2,1)} broadcast(bf16[]{:T(256)} %constant.50.clone.1), dimensions={} | broadcast | bytes 8388610 | tf_op jit(solution)/shard_map/broadcast_in_dim | solution.py:32
  153.6 20.7 %scatter_fusion = bf16[128,2,128,128]{3,2,1,0:T(8,128)(2,1)} fusion(bf16[128,2,128,128]{3,2,1,0:T(8,128)(2,1)} %broadcast_in_dim.5, s32[128]{0:T(128)S(1)} %fusion.26, bf16[128,128,128]{2,1,0:T(8,128)(2,1)} %bitcast.43), kind=kCustom, calls=%fused_computation | custom fusion | bytes 12583936 | tf_op jit(solution)/shard_map/scatter | solution.py:32
  174.4 5.4 %all-to-all-start = ((bf16[128,2,128,128]{3,2,1,0:T(8,128)(2,1)}), bf16[128,2,128,128]{3,2,1,0:T(8,128)(2,1)}, u32[]{:S(2)}, u32[]{:S(2)}) async-start(bf16[128,2,128,128]{3,2,1,0:T(8,128)(2,1)} %scatter_fusion), calls=%async_computation | async-start | bytes 16777216 | tf_op jit(solution)/shard_map/all_to_all | solution.py:34
  179.8 117.2 %all-gather = s32[32,32,4]{1,2,0:T(4,128)S(1)} all-gather(s32[1,32,4]{1,2,0:T(4,128)S(1)} %bitcast.47), channel_id=1, replica_groups=mesh['tok'=4,'vocab'=32] {'vocab'}, dimensions={0}, use_global_device_ids=true | all-gather | bytes 16896 | tf_op jit(solution)/shard_map/all_gather | solution.py:36
  297.2 1.3 convert_reduce_fusion
  298.7 10.1 %fusion.27 = (f32[512]{0:T(512)S(1)}, f32[512,1024]{1,0:T(8,128)}) fusion(bf16[512,4608]{1,0:T(8,128)(2,1)} %all-gather.3.cloned.1.call-done, bf16[4608,1024]{1,0:T(8,128)(2,1)} %param.8), kind=kOutput, calls=%fused_computation.64 | convolution fusion | flops 4832361984 | bytes 16254976 | tf_op jit(solution)/shard_map/dot_general | solution.py:50
  308.8 65.0 %pmax.15 = f32[512]{0:T(512)S(1)} all-reduce(f32[512]{0:T(512)S(1)} %get-tuple-element.24), channel_id=1, replica_groups=mesh['tok'=4,'vocab'=32] {'tok','vocab'}, use_global_device_ids=true, to_apply=%region_10.11 | all-reduce | flops 512 | bytes 4096 | tf_op jit(solution)/shard_map/pmax | solution.py:57
  373.9 8.9 %bitcast_reduce_fusion = (f32[4,128]{1,0:T(4,128)S(1)}, f32[4,128,128,8,1]{2,3,4,1,0:T(8,128)S(1)}) fusion(bf16[32,2,8,1,1]{2,1,0,4,3:T(2,128)(2,1)S(1)} %fusion.8, bf16[4,32,2,128,128]{4,3,2,1,0:T(8,128)(2,1)} %bitcast.5), kind=kOutput, calls=%fused_computation.14 | convolution fusion | flops 67632640 | bytes 10488832 | tf_op jit(solution)/shard_map/vcb,svctk->stbk/dot_general | solution.py:47
  382.8 1.2 fusion.6
  384.0 62.9 %all-reduce = (f32[512]{0:T(512)S(1)}, f32[512]{0:T(512)S(1)}, f32[512]{0:T(512)S(1)}, f32[512]{0:T(512)S(1)}) all-reduce(f32[512]{0:T(512)S(1)} %get-tuple-element.13, f32[512]{0:T(512)S(1)} %get-tuple-element.14, f32[512]{0:T(512)S(1)} %get-tuple-element.12, f32[512]{0:T(512)S(1)} %bitcast.46), channel_id=1, replica_groups=mesh['tok'=4,'vocab'=32] {'tok','vocab'}, use_global_device_ids=true, to_apply=%region_16.17 | all-reduce | flops 2048 | bytes 16384 | tf_op jit(solution)/shard_map/psum | solution.py:59
  446.8 10.9 %fusion.2 = bf16[4608,1024]{0,1:T(8,128)(2,1)} fusion(bf16[512,4608]{1,0:T(8,128)(2,1)} %all-gather.3.cloned.1.call-done, f32[512,1024]{1,0:T(8,128)} %get-tuple-element.25, f32[64,8,8,128]{3,2,1,0:T(8,128)S(1)} %bitcast.42, f32[512]{0:T(512)S(1)} %get-tuple-element.20, f32[512]{0:T(512)S(1)} %get-tuple-element.23, s32[1024]{0:T(1024)S(1)} %iota_add_fusion, ...), kind=kOutput, calls=%fused_computation.4 | convolution fusion | flops 4840226816 | bytes 18360320 | tf_op jit(solution)/shard_map/dot_general | solution.py:69
  457.8 12.6 %copy.54 = bf16[4608,1024]{1,0:T(8,128)(2,1)} copy(bf16[4608,1024]{0,1:T(8,128)(2,1)} %fusion.2) | data formatting | bytes 18874368
  470.4 0.6 dynamic_slice.3
  (24 shorter events, 0.8 us)
Async XLA Ops:
  7.2 68.0 %copy-start = (bf16[128,4096]{1,0:T(8,128)(2,1)S(1)}, bf16[128,4096]{1,0:T(8,128)(2,1)}, u32[]{:S(2)}) copy-start(bf16[128,4096]{1,0:T(8,128)(2,1)} %param.6) | copy-start | bytes 3145732
  7.2 291.5 %all-gather.3.cloned.1.call-start = ((), (), s32[]{:S(2)}) async-start(), calls=%async_computation.1 | async-start | bytes 5898240 | tf_op jit(solution)/shard_map/all_gather | solution.py:49
  142.7 2.2 copy-start.2
  174.4 5.4 %copy-start.4 = (s32[32,4]{0,1:T(4,128)S(1)}, s32[32,4]{0,1:T(4,128)}, u32[]{:S(2)}) copy-start(s32[32,4]{0,1:T(4,128)} %param.10) | copy-start | bytes 1540
  174.4 199.5 %all-to-all-start = ((bf16[128,2,128,128]{3,2,1,0:T(8,128)(2,1)}), bf16[128,2,128,128]{3,2,1,0:T(8,128)(2,1)}, u32[]{:S(2)}, u32[]{:S(2)}) async-start(bf16[128,2,128,128]{3,2,1,0:T(8,128)(2,1)} %scatter_fusion), calls=%async_computation | async-start | bytes 16777216 | tf_op jit(solution)/shard_map/all_to_all | solution.py:34
  373.8 8.9 %copy-start.1 = (f32[512,1024]{1,0:T(8,128)S(1)}, f32[512,1024]{1,0:T(8,128)}, u32[]{:S(2)}) copy-start(f32[512,1024]{1,0:T(8,128)} %get-tuple-element.25) | copy-start | bytes 6291460
  373.9 8.9 %copy-start.3 = (s32[512]{0:T(512)S(1)}, s32[512]{0:T(512)}, u32[]{:S(2)}) copy-start(s32[512]{0:T(512)} %param.9) | copy-start | bytes 6148
Sparse Core Ops, SparseCore 0:
  9.7 55.8 all-gather.2
where the time goes:
time: 479 us; the launch traced here: 478 us
  blocking collectives  377 us (79%)
  local copies, waits for them, and re-layouts  41.4 us (9%)
  matrix products  33.3 us (7%)
  between operations  14.2 us (3%)
  other arithmetic  5.87 us (1%)
  starting transfers between devices  5.46 us (1%)
    all_gather x1, blocking collectives, local(): lax.all_gather(map_target, 'vocab', axis=0, tiled=True)  117 us
    psum x1, blocking collectives, local(): lax.psum(jnp.sum(jnp.exp(scores - highest[:, None]), axis=1), 'vocab')  67 us
    pmax x1, blocking collectives, local(): top_all = lax.pmax(row_top, ('tok', 'vocab'))  65 us
    pmax x1, blocking collectives, local(): highest = lax.pmax(local_top, 'vocab')  64.8 us
    psum x1, blocking collectives, local(): lax.psum((exp_part, mass_part, inner_part, label_part), ('tok', 'vocab'))  62.9 us
    scatter x1, local copies, waits for them, and re-layouts, local(): jnp.zeros((nodes, capacity, tok_rows, block), jnp.bfloat16)  20.7 us
    unnamed x12, local copies, waits for them, and re-layouts  14.1 us
    dot_general x1, matrix products, local(): lax.dot_general(everyone, grad_logits, (((0,), (0,)), ((), ())), preferre...  10.9 us
  transfers between devices with their start and end apart: 2, of which 0 were waited for; matrix products, arithmetic and copies ran while one was open for 9% of the time, Pallas kernels for 0%

commit v1 on v0

--- a/solution.py
+++ b/solution.py
@@ -20,7 +20,9 @@
     scores = teacher_logits.astype(jnp.float32)
     local_top = jnp.max(scores, axis=1)
     highest = lax.pmax(local_top, "vocab")
-    total = lax.psum(jnp.sum(jnp.exp(scores - highest[:, None]), axis=1), "vocab")
+    own = jnp.sum(jnp.exp(scores - highest[:, None]), axis=1)
+    terms = lax.all_gather(own, "vocab", axis=0, tiled=False)
+    total = terms.sum(axis=0)
     teacher_prob = (jnp.exp(scores - highest[:, None]) / total[:, None]).astype(jnp.bfloat16)
     pieces = teacher_prob.reshape(tok_rows, old_blocks, block)
     contrib = jnp.einsum("tjb,jkbc->jktc", pieces, map_weight, preferred_element_type=jnp.float32)

time: 479 us -> 438 us (0.914)
  blocking collectives: 377 us -> 332 us
    psum x1 -> x0, blocking collectives: 67 us -> none  [local(): lax.psum(jnp.sum(jnp.exp(scores - highest[:, None]), axis=1), 'vocab')]
    all_gather x0 -> x1, blocking collectives: none -> 22.2 us  [local(): terms = lax.all_gather(own, 'vocab', axis=0, tiled=False)]
  transfers between devices with their start and end apart: 2 -> 2, of which waited for: 0 -> 0; matrix products, arithmetic and copies ran while one was open for 9% -> 10% of each run, Pallas kernels for 0% -> 0%
where the time goes in v1:
time: 438 us; the launch traced here: 437 us
  blocking collectives  332 us (76%)
  local copies, waits for them, and re-layouts  41.4 us (9%)
  matrix products  33.3 us (8%)
  between operations  14.2 us (3%)
  starting transfers between devices  9.62 us (2%)
  other arithmetic  5.92 us (1%)
    all_gather x1, blocking collectives, local(): lax.all_gather(map_target, 'vocab', axis=0, tiled=True)  117 us
    pmax x1, blocking collectives, local(): highest = lax.pmax(local_top, 'vocab')  64.8 us
    pmax x1, blocking collectives, local(): top_all = lax.pmax(row_top, ('tok', 'vocab'))  64.4 us
    psum x1, blocking collectives, local(): lax.psum((exp_part, mass_part, inner_part, label_part), ('tok', 'vocab'))  63.1 us
    all_gather x1, blocking collectives, local(): terms = lax.all_gather(own, 'vocab', axis=0, tiled=False)  22.2 us
    scatter x1, local copies, waits for them, and re-layouts, local(): jnp.zeros((nodes, capacity, tok_rows, block), jnp.bfloat16)  20.7 us
    unnamed x12, local copies, waits for them, and re-layouts  14.1 us
    dot_general x1, matrix products, local(): lax.dot_general(everyone, grad_logits, (((0,), (0,)), ((), ())), preferre...  11 us
  transfers between devices with their start and end apart: 2, of which 0 were waited for; matrix products, arithmetic and copies ran while one was open for 10% of the time, Pallas kernels for 0%

profile of v1, /device:TPU:1, one launch (start us, length us, event | category | flops | bytes accessed | tf_op | source)
XLA Modules:
  0.0 437.0 jit_solution(477236080882885919)
XLA Ops:
  7.2 0.7 all-gather.5.cloned.1.call-update
  7.9 0.7 add_select_fusion.2
  8.9 1.5 reduce_max.23
  10.4 64.8 %pmax.14 = f32[128]{0:T(128)S(1)} all-reduce(bf16[128]{0:T(256)(128)(2,1)S(1)} %reduce_max.23), channel_id=1, replica_groups=mesh['tok'=4,'vocab'=32] {'vocab'}, use_global_device_ids=true, to_apply=%region_2.0 | all-reduce | flops 128 | bytes 768 | tf_op jit(solution)/shard_map/pmax | solution.py:22
  75.2 0.5 fusion.7
  75.7 22.2 %all-gather.1 = f32[32,1,128]{2,1,0:T(1,128)S(1)} all-gather(f32[1,1,128]{2,1,0:T(1,128)S(1)} %bitcast.49), channel_id=2, replica_groups=mesh['tok'=4,'vocab'=32] {'vocab'}, dimensions={0}, use_global_device_ids=true | all-gather | bytes 16896 | tf_op jit(solution)/shard_map/all_gather | solution.py:24
  97.9 0.5 fusion.9
  98.4 0.2 copy.62
  98.7 0.2 convert_reduce_fusion.1
  98.8 1.3 copy-done.2
  100.1 3.2 convolution_convert_fusion.1
  103.3 5.5 %broadcast_in_dim.5 = bf16[128,2,128,128]{3,2,1,0:T(8,128)(2,1)} broadcast(bf16[]{:T(256)} %constant.50.clone.1), dimensions={} | broadcast | bytes 8388610 | tf_op jit(solution)/shard_map/broadcast_in_dim | solution.py:34
  108.8 20.7 %scatter_fusion = bf16[128,2,128,128]{3,2,1,0:T(8,128)(2,1)} fusion(bf16[128,2,128,128]{3,2,1,0:T(8,128)(2,1)} %broadcast_in_dim.5, s32[128]{0:T(128)S(1)} %fusion.26, bf16[128,128,128]{2,1,0:T(8,128)(2,1)} %bitcast.44), kind=kCustom, calls=%fused_computation | custom fusion | bytes 12583936 | tf_op jit(solution)/shard_map/scatter | solution.py:34
  129.6 9.6 %all-to-all-start = ((bf16[128,2,128,128]{3,2,1,0:T(8,128)(2,1)}), bf16[128,2,128,128]{3,2,1,0:T(8,128)(2,1)}, u32[]{:S(2)}, u32[]{:S(2)}) async-start(bf16[128,2,128,128]{3,2,1,0:T(8,128)(2,1)} %scatter_fusion), calls=%async_computation | async-start | bytes 16777216 | tf_op jit(solution)/shard_map/all_to_all | solution.py:36
  139.2 117.3 %all-gather.2 = s32[32,32,4]{1,2,0:T(4,128)S(1)} all-gather(s32[1,32,4]{1,2,0:T(4,128)S(1)} %bitcast.48), channel_id=1, replica_groups=mesh['tok'=4,'vocab'=32] {'vocab'}, dimensions={0}, use_global_device_ids=true | all-gather | bytes 16896 | tf_op jit(solution)/shard_map/all_gather | solution.py:38
  256.7 1.3 convert_reduce_fusion
  258.2 10.1 %fusion.27 = (f32[512]{0:T(512)S(1)}, f32[512,1024]{1,0:T(8,128)}) fusion(bf16[512,4608]{1,0:T(8,128)(2,1)} %all-gather.5.cloned.1.call-done, bf16[4608,1024]{1,0:T(8,128)(2,1)} %param.8), kind=kOutput, calls=%fused_computation.64 | convolution fusion | flops 4832361984 | bytes 16254976 | tf_op jit(solution)/shard_map/dot_general | solution.py:52
  268.3 64.4 %pmax.15 = f32[512]{0:T(512)S(1)} all-reduce(f32[512]{0:T(512)S(1)} %get-tuple-element.24), channel_id=1, replica_groups=mesh['tok'=4,'vocab'=32] {'tok','vocab'}, use_global_device_ids=true, to_apply=%region_10.11 | all-reduce | flops 512 | bytes 4096 | tf_op jit(solution)/shard_map/pmax | solution.py:59
  332.7 8.9 %bitcast_reduce_fusion = (f32[4,128]{1,0:T(4,128)S(1)}, f32[4,128,128,8,1]{2,3,4,1,0:T(8,128)S(1)}) fusion(bf16[32,2,8,1,1]{2,1,0,4,3:T(2,128)(2,1)S(1)} %fusion.8, bf16[4,32,2,128,128]{4,3,2,1,0:T(8,128)(2,1)} %bitcast.6), kind=kOutput, calls=%fused_computation.14 | convolution fusion | flops 67632640 | bytes 10488832 | tf_op jit(solution)/shard_map/vcb,svctk->stbk/dot_general | solution.py:49
  341.7 1.2 fusion.6
  342.9 63.1 %all-reduce = (f32[512]{0:T(512)S(1)}, f32[512]{0:T(512)S(1)}, f32[512]{0:T(512)S(1)}, f32[512]{0:T(512)S(1)}) all-reduce(f32[512]{0:T(512)S(1)} %get-tuple-element.13, f32[512]{0:T(512)S(1)} %get-tuple-element.14, f32[512]{0:T(512)S(1)} %get-tuple-element.12, f32[512]{0:T(512)S(1)} %bitcast.47), channel_id=1, replica_groups=mesh['tok'=4,'vocab'=32] {'tok','vocab'}, use_global_device_ids=true, to_apply=%region_16.17 | all-reduce | flops 2048 | bytes 16384 | tf_op jit(solution)/shard_map/psum | solution.py:61
  406.0 11.0 %fusion.2 = bf16[4608,1024]{0,1:T(8,128)(2,1)} fusion(bf16[512,4608]{1,0:T(8,128)(2,1)} %all-gather.5.cloned.1.call-done, f32[512,1024]{1,0:T(8,128)} %get-tuple-element.25, f32[64,8,8,128]{3,2,1,0:T(8,128)S(1)} %bitcast.43, f32[512]{0:T(512)S(1)} %get-tuple-element.20, f32[512]{0:T(512)S(1)} %get-tuple-element.23, s32[1024]{0:T(1024)S(1)} %iota_add_fusion, ...), kind=kOutput, calls=%fused_computation.4 | convolution fusion | flops 4840226816 | bytes 18360320 | tf_op jit(solution)/shard_map/dot_general | solution.py:71
  417.0 12.6 %copy.54 = bf16[4608,1024]{1,0:T(8,128)(2,1)} copy(bf16[4608,1024]{0,1:T(8,128)(2,1)} %fusion.2) | data formatting | bytes 18874368
  429.6 0.6 dynamic_slice.3
  (25 shorter events, 0.8 us)
Async XLA Ops:
  7.2 68.0 %copy-start = (bf16[128,4096]{1,0:T(8,128)(2,1)S(1)}, bf16[128,4096]{1,0:T(8,128)(2,1)}, u32[]{:S(2)}) copy-start(bf16[128,4096]{1,0:T(8,128)(2,1)} %param.6) | copy-start | bytes 3145732
  7.2 251.0 %all-gather.5.cloned.1.call-start = ((), (), s32[]{:S(2)}) async-start(), calls=%async_computation.1 | async-start | bytes 5898240 | tf_op jit(solution)/shard_map/all_gather | solution.py:51
  97.9 2.2 copy-start.2
  129.6 9.6 %copy-start.4 = (s32[32,4]{0,1:T(4,128)S(1)}, s32[32,4]{0,1:T(4,128)}, u32[]{:S(2)}) copy-start(s32[32,4]{0,1:T(4,128)} %param.10) | copy-start | bytes 1540
  129.6 203.2 %all-to-all-start = ((bf16[128,2,128,128]{3,2,1,0:T(8,128)(2,1)}), bf16[128,2,128,128]{3,2,1,0:T(8,128)(2,1)}, u32[]{:S(2)}, u32[]{:S(2)}) async-start(bf16[128,2,128,128]{3,2,1,0:T(8,128)(2,1)} %scatter_fusion), calls=%async_computation | async-start | bytes 16777216 | tf_op jit(solution)/shard_map/all_to_all | solution.py:36
  332.7 8.9 %copy-start.1 = (f32[512,1024]{1,0:T(8,128)S(1)}, f32[512,1024]{1,0:T(8,128)}, u32[]{:S(2)}) copy-start(f32[512,1024]{1,0:T(8,128)} %get-tuple-element.25) | copy-start | bytes 6291460
  332.7 8.9 %copy-start.3 = (s32[512]{0:T(512)S(1)}, s32[512]{0:T(512)}, u32[]{:S(2)}) copy-start(s32[512]{0:T(512)} %param.9) | copy-start | bytes 6148
Sparse Core Ops, SparseCore 0:
  9.7 55.8 all-gather.4
